TPU v7x, 32 devices: a whole 2x2x4 slice. The times are simulated.
32 devices in a mesh: groups: 2 (over y), inst: 4 (over z), tp: 4 (over x, core).
Axes of the slice: x: 2, y: 2, z: 4, core: 2. Of those that a mesh axis runs over, the one named last changes fastest.
Arguments:
- hidden: bfloat16 [192, 32, 5120], P(('groups', 'inst'), None, 'tp'), parts along dimension 0, may hold values from -400 to 400
- norm_gain: float32 [5120], replicated, may hold values from 0.1 to 1.9
- w_query: bfloat16 [5120, 4096], P('inst', 'tp'), may hold values from -0.078125 to 0.078125
- w_key: bfloat16 [5120, 512], P('inst', 'tp'), may hold values from -0.078125 to 0.078125
- w_value: bfloat16 [5120, 512], P('inst', 'tp'), may hold values from -0.078125 to 0.078125
- bias_query: float32 [4096], P('tp'), may hold values from -3 to 3
- bias_key: float32 [512], P('tp'), may hold values from -81 to 81
- bias_value: float32 [512], P('tp'), may hold values from -3 to 3
- prefix_blocks: int32 [8], P(('groups', 'inst')), parts along dimension 0, may hold values from 1 to 24, as said below
- block_target: int32 [8, 24], P(('groups', 'inst')), parts along dimension 0, may hold values from -1 to 47, as said below
- cache_slot: int32 [8, 24], P(('groups', 'inst')), parts along dimension 0, may hold values from 0 to 23, each once within a row
Outputs:
- attn_out: bfloat16 [96, 32, 4096], P(('groups', 'inst'), None, 'tp'), parts along dimension 0
- key_cache: bfloat16 [192, 32, 512], P(('groups', 'inst'), None, 'tp'), parts along dimension 0
- value_cache: bfloat16 [192, 32, 512], P(('groups', 'inst'), None, 'tp'), parts along dimension 0
There are 2 independent parts, one for each index of `groups`. A program takes and returns all parts, laid end to end along the dimension named above; an argument that names none is the same for every part. Nothing has to cross between parts.
Inputs may be any that keep to these rules, and one draw needn't show every extreme that they name: `prefix_blocks`: some instance holds 24 blocks; all prefixes together hold exactly 48 blocks. `block_target`: for a live slot, b * 12 + c names slot c of balancing instance b; dead slots hold -1. Every balancing slot is named exactly once. No instance sends more than 6 blocks to one balancing instance, and in every draw some instance sends exactly 6 to some balancing instance.
All inputs are finite; a program needn't handle non-finite values.
Results may differ from a plain program's by a relative error of at most 0.0018.
The roundings to bfloat16 on the way count: a program that leaves them out, or rounds other values in their place, can miss the bound.
Values may be sent and summed in bfloat16 or wider, within the bound.
A program may use at most 128 MiB of HBM per device.

v0:
```python
import math

import jax
import jax.numpy as jnp
from jax import lax
from jax.sharding import PartitionSpec as P

HD = 128
BAL = 12


ROPE_BASE = 1000000.0
NORM_EPS = 1e-06


def rotate(values, positions):
    width = values.shape[-1]
    half = width // 2
    freqs = ROPE_BASE ** (-(jnp.arange(half, dtype=jnp.float32) * 2.0 / width))
    angles = positions.astype(jnp.float32)[:, None] * freqs[None, :]
    cosine = jnp.cos(angles)[:, None, :]
    sine = jnp.sin(angles)[:, None, :]
    first = values[..., :half]
    second = values[..., half:]
    return jnp.concatenate(
        [first * cosine - second * sine, second * cosine + first * sine], axis=-1
    )


def project(whole, positions, norm_gain, w_query, w_key, w_value, bias_query, bias_key, bias_value):
    values = whole.astype(jnp.float32)
    inverse_rms = lax.rsqrt(jnp.mean(values * values, axis=-1, keepdims=True) + NORM_EPS)
    normed = (values * inverse_rms * norm_gain).astype(jnp.bfloat16)
    total_rows = normed.shape[0]
    query_sum = jnp.dot(
        normed,
        lax.all_gather(w_query, "inst", axis=0, tiled=True),
        preferred_element_type=jnp.float32,
    )
    key_sum = jnp.dot(
        normed,
        lax.all_gather(w_key, "inst", axis=0, tiled=True),
        preferred_element_type=jnp.float32,
    )
    value_sum = jnp.dot(
        normed,
        lax.all_gather(w_value, "inst", axis=0, tiled=True),
        preferred_element_type=jnp.float32,
    )
    query = query_sum
    keys = key_sum
    vals = value_sum
    query = rotate((query + bias_query).reshape(total_rows, -1, HD), positions)
    query = query.reshape(total_rows, -1).astype(jnp.bfloat16)
    keys = rotate((keys + bias_key).reshape(total_rows, -1, HD), positions)
    keys = keys.reshape(total_rows, -1).astype(jnp.bfloat16)
    vals = (vals + bias_value).astype(jnp.bfloat16)
    return (query, keys, vals)


def pick_slots(labels_place, labels_live, count):
    items = jnp.arange(labels_place.shape[0], dtype=jnp.int32)
    wanted = (labels_place[None, :] == jnp.arange(count, dtype=jnp.int32)[:, None]) & (
        labels_live[None, :] == 1
    )
    return jnp.sum(jnp.where(wanted, items[None, :], 0), axis=1)


def shards(
    hidden,
    norm_gain,
    w_query,
    w_key,
    w_value,
    bias_query,
    bias_key,
    bias_value,
    prefix_blocks,
    block_target,
    cache_slot,
):
    owned, width_block, part_width = hidden.shape
    peers = lax.axis_size("inst")
    pair = -(-owned // peers)
    total_rows = owned * width_block
    slots = jnp.arange(owned, dtype=jnp.int32)
    live = slots < prefix_blocks[0]
    target = block_target[0]
    dest = jnp.where(live, target // BAL, -1)
    place = jnp.where(live, target % BAL, 0)
    earlier = (dest[:, None] == dest[None, :]) & live[None, :] & (slots[None, :] < slots[:, None])
    rank = jnp.sum(earlier.astype(jnp.int32), axis=1)
    item_of_slot = jnp.where(live, dest * pair + rank, -1)
    items = jnp.arange(peers * pair, dtype=jnp.int32)
    matched = item_of_slot[None, :] == items[:, None]
    present = jnp.any(matched, axis=1)
    source = jnp.sum(jnp.where(matched, slots[None, :], 0), axis=1)
    own_positions = jnp.arange(total_rows, dtype=jnp.int32)
    zero_half = jnp.zeros((), jnp.bfloat16)
    whole = lax.all_gather(hidden.reshape(total_rows, part_width), "tp", axis=1, tiled=True)
    query, keys, vals = project(
        whole, own_positions, norm_gain, w_query, w_key, w_value, bias_query, bias_key, bias_value
    )
    kv_here = keys.shape[1] // HD
    group = query.shape[1] // (HD * kv_here)
    query_heads = query.reshape(total_rows, kv_here, group, HD)
    key_heads = keys.reshape(total_rows, kv_here, HD)
    value_heads = vals.reshape(total_rows, kv_here, HD)
    causal = own_positions[:, None] >= own_positions[None, :]
    scale_factor = 1.0 / math.sqrt(HD)

    def head(query_group):
        scores = (
            jnp.einsum("rkd,skd->krs", query_group, key_heads, preferred_element_type=jnp.float32)
            * scale_factor
        )
        scores = jnp.where(causal[None], scores, -jnp.inf)
        largest = jnp.max(scores, axis=-1, keepdims=True)
        expo = jnp.exp(scores - largest)
        probs = (expo / jnp.sum(expo, axis=-1, keepdims=True)).astype(jnp.bfloat16)
        mixed = jnp.einsum("krs,skd->rkd", probs, value_heads, preferred_element_type=jnp.float32)
        return mixed.astype(jnp.bfloat16)

    heads_out = lax.map(head, jnp.moveaxis(query_heads, 2, 0))
    attention = jnp.transpose(heads_out, (1, 2, 0, 3)).reshape(owned, width_block, -1)
    perm = cache_slot[0]
    inverse = jnp.sum(jnp.where(perm[None, :] == slots[:, None], slots[None, :], 0), axis=1)
    live_blocks = live[:, None, None]
    key_blocks = jnp.where(live_blocks, keys.reshape(owned, width_block, -1), zero_half)
    value_blocks = jnp.where(live_blocks, vals.reshape(owned, width_block, -1), zero_half)
    key_cache = jnp.take(key_blocks, inverse, axis=0)
    value_cache = jnp.take(value_blocks, inverse, axis=0)
    send_out = jnp.where(present[:, None, None], jnp.take(attention, source, axis=0), zero_half)
    send_out = send_out.reshape(peers, pair, width_block, -1)
    out_labels = jnp.stack([jnp.take(place, source), present.astype(jnp.int32)], axis=-1).reshape(
        peers, pair, 2
    )
    got_out, got_out_labels = (
        lax.all_to_all(send_out, "inst", split_axis=0, concat_axis=0, tiled=True),
        lax.all_to_all(out_labels, "inst", split_axis=0, concat_axis=0, tiled=True),
    )
    got_out = got_out.reshape(peers * pair, width_block, -1)
    got_out_labels = got_out_labels.reshape(peers * pair, 2)
    chosen_out = pick_slots(got_out_labels[:, 0], got_out_labels[:, 1], BAL)
    attn_out = jnp.take(got_out, chosen_out, axis=0)
    return (attn_out, key_cache, value_cache)


def solution(mesh):
    in_specs = (
        P(("groups", "inst"), None, "tp"),
        P(),
        P("inst", "tp"),
        P("inst", "tp"),
        P("inst", "tp"),
        P("tp"),
        P("tp"),
        P("tp"),
        P(("groups", "inst")),
        P(("groups", "inst"), None),
        P(("groups", "inst"), None),
    )
    out_specs = (
        P(("groups", "inst"), None, "tp"),
        P(("groups", "inst"), None, "tp"),
        P(("groups", "inst"), None, "tp"),
    )
    return jax.shard_map(shards, mesh=mesh, in_specs=in_specs, out_specs=out_specs, check_vma=False)
```

profile of v0, /device:TPU:0, one launch (start us, length us, event | category | flops | bytes accessed | tf_op | source)
XLA Modules:
  0.0 404.3 jit_solution(11902307673242305286)
XLA Ops:
  7.2 0.7 all-gather.5.cloned.1.call-update
  7.9 0.7 all-gather.9.cloned.1.call-update
  8.7 0.7 all-gather.11.cloned.1.call-update
  9.4 0.5 all-gather.7.cloned.1.call-update
  11.1 0.7 gather_fusion
  12.1 0.6 copy.34
  12.7 6.3 %all-to-all-start = ((s32[4,6,2]{1,2,0:T(2,128)}), s32[4,6,2]{1,2,0:T(2,128)S(1)}, u32[]{:S(2)}, u32[]{:S(2)}) async-start(s32[4,6,2]{1,2,0:T(2,128)} %copy.34), calls=%async_computation | async-start | bytes 8192 | tf_op jit(solution)/shard_map/all_to_all | solution.py:140
  19.1 0.6 broadcast_in_dim.138
  19.8 0.8 multiply_cosine_fusion.1
  20.6 47.0 %all-gather.5.cloned.1.call-done = bf16[768,5120]{1,0:T(8,128)(2,1)} async-done(((bf16[768,1280]{1,0:T(8,128)(2,1)}), bf16[768,5120]{1,0:T(8,128)(2,1)}) %all-gather.5.cloned.1.call-update) | async-done | bytes 7864336 | tf_op jit(solution)/shard_map/all_gather | solution.py:100
  67.6 4.8 %fusion.12 = f32[768]{0:T(1024)S(1)} fusion(bf16[768,5120]{1,0:T(8,128)(2,1)} %all-gather.5.cloned.1.call-done), kind=kLoop, calls=%fused_computation.22 | loop fusion | flops 11795712 | bytes 7867392 | tf_op jit(solution)/shard_map/reduce_sum | solution.py:32
  72.5 29.5 %all-gather.9.cloned.1.call-done = bf16[5120,128]{1,0:T(8,128)(2,1)} async-done(((bf16[1280,128]{1,0:T(8,128)(2,1)}), bf16[5120,128]{1,0:T(8,128)(2,1)}) %all-gather.9.cloned.1.call-update) | async-done | bytes 1310736 | tf_op jit(solution)/shard_map/all_gather | solution.py:42
  101.9 6.5 %fusion.15 = f32[768,1,128]{0,2,1:T(8,128)S(1)} fusion(bf16[5120,128]{1,0:T(8,128)(2,1)} %all-gather.9.cloned.1.call-done, f32[128]{0:T(128)S(1)} %copy-done.6, bf16[768,5120]{1,0:T(8,128)(2,1)} %all-gather.5.cloned.1.call-done, f32[5120]{0:T(1024)S(1)} %copy-done.4, f32[768]{0:T(1024)S(1)} %add_rsqrt_fusion), kind=kOutput, calls=%fused_computation.32 | convolution fusion | flops 1022459904 | bytes 9592320 | tf_op jit(solution)/shard_map/dot_general | solution.py:40
  108.4 0.8 fusion.23
  109.2 0.8 copy.39
  110.1 25.2 %all-gather.11.cloned.1.call-done = bf16[5120,128]{1,0:T(8,128)(2,1)} async-done(((bf16[1280,128]{1,0:T(8,128)(2,1)}), bf16[5120,128]{1,0:T(8,128)(2,1)}) %all-gather.11.cloned.1.call-update) | async-done | bytes 1310736 | tf_op jit(solution)/shard_map/all_gather | solution.py:47
  135.2 6.6 %fusion.16 = bf16[768,128]{1,0:T(8,128)(2,1)} fusion(bf16[5120,128]{1,0:T(8,128)(2,1)} %all-gather.11.cloned.1.call-done, f32[128]{0:T(128)S(1)} %copy-done.7, bf16[768,5120]{1,0:T(8,128)(2,1)} %all-gather.5.cloned.1.call-done, f32[5120]{0:T(1024)S(1)} %copy-done.4, f32[768]{0:T(1024)S(1)} %add_rsqrt_fusion), kind=kOutput, calls=%fused_computation.33 | convolution fusion | flops 1022558208 | bytes 9395712 | tf_op jit(solution)/shard_map/dot_general | solution.py:45
  141.8 177.8 %all-gather.7.cloned.1.call-done = bf16[5120,1024]{1,0:T(8,128)(2,1)} async-done(((bf16[1280,1024]{1,0:T(8,128)(2,1)}), bf16[5120,1024]{1,0:T(8,128)(2,1)}) %all-gather.7.cloned.1.call-update) | async-done | bytes 10485776 | tf_op jit(solution)/shard_map/all_gather | solution.py:37
  319.6 14.6 %convolution_add_fusion = f32[768,1024]{1,0:T(8,128)} fusion(bf16[5120,1024]{1,0:T(8,128)(2,1)} %all-gather.7.cloned.1.call-done, f32[1024]{0:T(1024)S(1)} %copy-done.5, bf16[768,5120]{1,0:T(8,128)(2,1)} %all-gather.5.cloned.1.call-done, f32[5120]{0:T(1024)S(1)} %copy-done.4, f32[768]{0:T(1024)S(1)} %add_rsqrt_fusion), kind=kOutput, calls=%fused_computation.25 | convolution fusion | flops 8069578752 | bytes 21523456 | tf_op jit(solution)/shard_map/dot_general | solution.py:35
  334.2 2.4 copy.42
  337.1 1.3 copy-done
  338.4 12.1 %while.11 = (s32[]{:T(128)}, bf16[8,768,1,128]{3,1,2,0:T(8,128)(2,1)S(1)}, bf16[8,768,1,128]{1,3,0,2:T(8,128)(2,1)S(1)}, bf16[768,1,128]{2,0,1:T(8,128)(2,1)S(1)}, bf16[768,1,128]{2,0,1:T(8,128)(2,1)S(1)}, /*index=5*/s32[]{:T(128)}) while((s32[]{:T(128)}, bf16[8,768,1,128]{3,1,2,0:T(8,128)(2,1)S(1)}, ...), condition=%wide.region_8.9_spmd.clone, body=%wide.region_5.8_spmd.clone.sunk | while | flops 307395072 | bytes 7881805 | solution.py:124
  339.3 0.6 fusion.49
  339.9 0.5 fusion.47
  340.8 0.6 fusion.49
  341.4 0.5 fusion.47
  342.3 0.6 fusion.49
  343.0 0.5 fusion.47
  343.8 0.6 fusion.49
  344.5 0.5 fusion.47
  345.3 0.6 fusion.49
  346.0 0.5 fusion.47
  346.8 0.6 fusion.49
  347.5 0.5 fusion.47
  348.4 0.6 fusion.49
  349.0 0.5 fusion.47
  349.9 0.6 fusion.49
  350.5 1.0 copy.40
  351.5 0.7 reshape.401
  352.3 0.6 gather_fusion.1
  352.9 2.1 select_select_fusion
  355.0 3.7 all-to-all-start.1
  359.3 0.6 gather_fusion.3
  359.8 0.6 gather_fusion.4
  360.4 0.8 broadcast_select_fusion.1
  361.3 34.9 %all-to-all-done.1 = bf16[4,6,32,1024]{3,2,1,0:T(8,128)(2,1)S(1)} async-done(((bf16[4,6,32,1024]{3,2,1,0:T(8,128)(2,1)}), bf16[4,6,32,1024]{3,2,1,0:T(8,128)(2,1)S(1)}, u32[]{:S(2)}, u32[]{:S(2)}) %all-to-all-start.1) | async-done | bytes 1572896 | tf_op jit(solution)/shard_map/all_to_all | solution.py:139
  396.2 0.6 gather_fusion.2
  396.8 1.0 broadcast_select_fusion
  (68 shorter events, 5.5 us)
Async XLA Ops:
  7.2 60.4 %all-gather.5.cloned.1.call-start = ((), (), s32[]{:S(2)}) async-start(), calls=%async_computation.2 | async-start | bytes 9830400 | tf_op jit(solution)/shard_map/all_gather | solution.py:100
  7.2 3.4 copy-start.3
  7.9 94.0 %all-gather.9.cloned.1.call-start = ((), (), s32[]{:S(2)}) async-start(), calls=%async_computation.4 | async-start | bytes 1638400 | tf_op jit(solution)/shard_map/all_gather | solution.py:42
  8.6 126.6 %all-gather.11.cloned.1.call-start = ((), (), s32[]{:S(2)}) async-start(), calls=%async_computation.5 | async-start | bytes 1638400 | tf_op jit(solution)/shard_map/all_gather | solution.py:47
  9.4 310.2 %all-gather.7.cloned.1.call-start = ((), (), s32[]{:S(2)}) async-start(), calls=%async_computation.3 | async-start | bytes 13107200 | tf_op jit(solution)/shard_map/all_gather | solution.py:37
  12.7 342.3 %all-to-all-start = ((s32[4,6,2]{1,2,0:T(2,128)}), s32[4,6,2]{1,2,0:T(2,128)S(1)}, u32[]{:S(2)}, u32[]{:S(2)}) async-start(s32[4,6,2]{1,2,0:T(2,128)} %copy.34), calls=%async_computation | async-start | bytes 8192 | tf_op jit(solution)/shard_map/all_to_all | solution.py:140
  20.5 81.4 %copy-start.4 = (f32[5120]{0:T(1024)S(1)}, f32[5120]{0:T(1024)}, u32[]{:S(2)}) copy-start(f32[5120]{0:T(1024)} %param.16) | copy-start | bytes 61444
  20.6 81.4 %copy-start.6 = (f32[128]{0:T(128)S(1)}, f32[128]{0:T(128)}, u32[]{:S(2)}) copy-start(f32[128]{0:T(128)} %param.21) | copy-start | bytes 1540
  72.4 62.8 %copy-start.7 = (f32[128]{0:T(128)S(1)}, f32[128]{0:T(128)}, u32[]{:S(2)}) copy-start(f32[128]{0:T(128)} %param.22) | copy-start | bytes 1540
  110.0 209.5 %copy-start.5 = (f32[1024]{0:T(1024)S(1)}, f32[1024]{0:T(1024)}, u32[]{:S(2)}) copy-start(f32[1024]{0:T(1024)} %param.20) | copy-start | bytes 12292
  337.0 1.4 copy-start
  337.0 1.4 copy-start.1
  337.0 1.4 copy-start.2
  355.0 3.7 copy-start.8
  355.0 41.1 %all-to-all-start.1 = ((bf16[4,6,32,1024]{3,2,1,0:T(8,128)(2,1)}), bf16[4,6,32,1024]{3,2,1,0:T(8,128)(2,1)S(1)}, u32[]{:S(2)}, u32[]{:S(2)}) async-start(bf16[4,6,32,1024]{3,2,1,0:T(8,128)(2,1)} %select_select_fusion), calls=%async_computation.1 | async-start | bytes 3145728 | tf_op jit(solution)/shard_map/all_to_all | solution.py:139
Sparse Core Ops, SparseCore 0:
  9.6 57.9 all-gather.4
  69.2 32.6 all-gather.8
  103.5 31.6 all-gather.10
  136.6 182.9 all-gather.6
where the time goes:
time: 405 us; the launch traced here: 404 us
  waiting for transfers between devices  317 us (78%)
  matrix products  36.6 us (9%)
  other arithmetic  14.7 us (4%)
  between operations  14.7 us (4%)
  local copies, waits for them, and re-layouts  11.1 us (3%)
  starting transfers between devices  10.2 us (3%)
    all_gather x1, waiting for transfers between devices, project(): lax.all_gather(w_query, 'inst', axis=0, tiled=True)  178 us
    all_gather x1, waiting for transfers between devices, shards(): lax.all_gather(hidden.reshape(total_rows, part_width), 'tp', axis=1, tile...  47 us
    all_to_all x1, waiting for transfers between devices, shards(): lax.all_to_all(send_out, 'inst', split_axis=0, concat_axis=0, tiled=True)  34.9 us
    all_gather x1, waiting for transfers between devices, project(): lax.all_gather(w_key, 'inst', axis=0, tiled=True)  29.5 us
    all_gather x1, waiting for transfers between devices, project(): lax.all_gather(w_value, 'inst', axis=0, tiled=True)  25.2 us
    dot_general x1, matrix products, project(): jnp.dot(normed, lax.all_gather(w_query, 'inst', axis=0, tiled=True), pref...  14.6 us
  transfers between devices with their start and end apart: 6, of which 5 were waited for; matrix products, arithmetic and copies ran while one was open for 15% of the time, Pallas kernels for 0%

commit v1 on v0

--- a/solution.py
+++ b/solution.py
@@ -1,8 +1,11 @@
+import functools
 import math
 
 import jax
 import jax.numpy as jnp
 from jax import lax
+from jax.experimental import pallas as pl
+from jax.experimental.pallas import tpu as pltpu
 from jax.sharding import PartitionSpec as P
 
 HD = 128
@@ -146,7 +149,456 @@
     return (attn_out, key_cache, value_cache)
 
 
+TILE = 256
+PIECE = 256
+MESH = pl.DeviceIdType.MESH
+
+
+def fused_kernel(
+    n,
+    tp,
+    pair,
+    source_ref,
+    hid_ref,
+    wq_ref,
+    wk_ref,
+    wv_ref,
+    gain_ref,
+    bias_ref,
+    cos_ref,
+    sin_ref,
+    lab_ref,
+    key_ref,
+    val_ref,
+    got_ref,
+    lab_out,
+    hbuf,
+    normed,
+    wfull,
+    qbuf,
+    atb,
+    sendbuf,
+    loc_sem,
+    h_send,
+    h_recv,
+    z_send,
+    z_recv,
+    y_send,
+    y_recv,
+    d_send,
+    d_recv,
+    l_send,
+    l_recv,
+):
+    g = lax.axis_index("groups")
+    i = lax.axis_index("inst")
+    t = lax.axis_index("tp")
+    x, core = t // 2, t % 2
+    t_core = 2 * x + (1 - core)
+    t_far = 2 * (1 - x) + core
+    t_diag = 2 * (1 - x) + (1 - core)
+    tokens, part = hid_ref.shape
+    rows = wq_ref.shape[0]
+    half = rows // 2
+    pieces = wfull.shape[0]
+    peers_inst = [b for b in range(n)]
+
+    local = [pltpu.make_async_copy(hid_ref, hbuf.at[t], loc_sem.at[0])]
+    own = pl.ds(pl.multiple_of(i * rows, rows), rows)
+    local.append(pltpu.make_async_copy(wk_ref, wfull.at[0, own, pl.ds(0, HD)], loc_sem.at[1]))
+    local.append(pltpu.make_async_copy(wv_ref, wfull.at[0, own, pl.ds(HD, HD)], loc_sem.at[2]))
+    for c in range(1, pieces):
+        local.append(
+            pltpu.make_async_copy(
+                wq_ref.at[:, pl.ds((c - 1) * PIECE, PIECE)], wfull.at[c, own], loc_sem.at[c + 2]
+            )
+        )
+    for copy in local:
+        copy.start()
+
+    barrier = pltpu.get_barrier_semaphore()
+    for b in peers_inst:
+
+        @pl.when(i != b)
+        def _():
+            pl.semaphore_signal(barrier, inc=1, device_id=(g, b, t), device_id_type=MESH)
+
+    for other in ((1 - g, i, t), (g, i, t_core), (g, i, t_far)):
+        pl.semaphore_signal(barrier, inc=1, device_id=other, device_id_type=MESH)
+    pl.semaphore_wait(barrier, n - 1 + 3)
+
+    pending = []
+
+    def start(cond, make):
+        pending.append((cond, make))
+        if cond is None:
+            make().start()
+        else:
+
+            @pl.when(cond)
+            def _():
+                make().start()
+
+    def arrive(cond, make):
+        @pl.when(cond)
+        def _():
+            make().wait_recv()
+
+    def piece(c, j, h):
+        return wfull.at[c, pl.ds(pl.multiple_of(j * rows + h * half, half), half)]
+
+    def z_copy(c, d, s, j):
+        to = i + 1 if d == 0 else i - 1
+        return pltpu.make_async_remote_copy(
+            src_ref=piece(c, j, g),
+            dst_ref=piece(c, j, g),
+            send_sem=z_send.at[c, d, s],
+            recv_sem=z_recv.at[c, d, s],
+            device_id=(g, to, t),
+            device_id_type=MESH,
+        )
+
+    def y_copy(c, d, s, j, h):
+        return pltpu.make_async_remote_copy(
+            src_ref=piece(c, j, h),
+            dst_ref=piece(c, j, h),
+            send_sem=y_send.at[c, d, s],
+            recv_sem=y_recv.at[c, d, s],
+            device_id=(1 - g, i, t),
+            device_id_type=MESH,
+        )
+
+    def hid_copy(k, slot, to):
+        return pltpu.make_async_remote_copy(
+            src_ref=hbuf.at[slot],
+            dst_ref=hbuf.at[slot],
+            send_sem=h_send.at[k],
+            recv_sem=h_recv.at[k],
+            device_id=(g, i, to),
+            device_id_type=MESH,
+        )
+
+    def send_z(c, s):
+        start((i - s >= 0) & (i < n - 1), functools.partial(z_copy, c, 0, s, i - s))
+        start((i + s <= n - 1) & (i > 0), functools.partial(z_copy, c, 1, s, i + s))
+
+    def comm(c):
+        for s in range(n - 1):
+            for d in range(2):
+                j = i - 1 - s if d == 0 else i + 1 + s
+                have = j >= 0 if d == 0 else j <= n - 1
+                arrive(have, functools.partial(z_copy, c, d, s, j))
+                if s + 1 < n - 1:
+                    onward = have & ((i < n - 1) if d == 0 else (i > 0))
+                    start(onward, functools.partial(z_copy, c, d, s + 1, j))
+                start(have, functools.partial(y_copy, c, d, s, j, g))
+
+    def settle(c):
+        for s in range(n - 1):
+            for d in range(2):
+                j = i - 1 - s if d == 0 else i + 1 + s
+                have = j >= 0 if d == 0 else j <= n - 1
+                arrive(have, functools.partial(y_copy, c, d, s, j, 1 - g))
+
+    def norm():
+        @pl.loop(0, tokens // 32)
+        def _(r):
+            here = pl.ds(pl.multiple_of(r * 32, 32), 32)
+            total = jnp.zeros((32, 1), jnp.float32)
+            for p in range(tp):
+                v = hbuf[p, here, :].astype(jnp.float32)
+                total = total + jnp.sum(v * v, axis=-1, keepdims=True)
+            inverse = lax.rsqrt(total / (tp * part) + NORM_EPS)
+            for p in range(tp):
+                cols = pl.ds(p * part, part)
+                v = hbuf[p, here, :].astype(jnp.float32)
+                normed[here, cols] = (v * inverse * gain_ref[:, cols]).astype(jnp.bfloat16)
+
+    def turn(v, here):
+        return v * cos_ref[here, :] + pltpu.roll(v, HD // 2, 1) * sin_ref[here, :]
+
+    def product(c):
+        @pl.loop(0, tokens // TILE)
+        def _(r):
+            here = pl.ds(pl.multiple_of(r * TILE, TILE), TILE)
+            acc = jnp.dot(normed[here, :], wfull[c], preferred_element_type=jnp.float32)
+            acc = acc + bias_ref[:, pl.ds(c * PIECE, PIECE)]
+            first, second = acc[:, :HD], acc[:, HD:]
+            if c == 0:
+                key_ref[here, :] = turn(first, here).astype(jnp.bfloat16)
+                val_ref[here, :] = second.astype(jnp.bfloat16)
+            else:
+                qbuf[here, pl.ds(0, HD)] = turn(first, here).astype(jnp.bfloat16)
+                qbuf[here, pl.ds(HD, HD)] = turn(second, here).astype(jnp.bfloat16)
+
+    def attend():
+        scale = 1.0 / math.sqrt(HD)
+        rr = lax.broadcasted_iota(jnp.int32, (TILE, TILE), 0)
+        cc = lax.broadcasted_iota(jnp.int32, (TILE, TILE), 1)
+        block = atb.shape[1]
+        for r in range(tokens // TILE):
+            for head in range(PIECE // HD):
+                q = qbuf[pl.ds(r * TILE, TILE), pl.ds(head * HD, HD)]
+                width = (r + 1) * TILE
+                sc = (
+                    lax.dot_general(
+                        q,
+                        key_ref[pl.ds(0, width), :],
+                        (((1,), (1,)), ((), ())),
+                        preferred_element_type=jnp.float32,
+                    )
+                    * scale
+                )
+                last = jnp.where(rr >= cc, sc[:, width - TILE :], -jnp.inf)
+                sc = last if r == 0 else jnp.concatenate([sc[:, : width - TILE], last], axis=1)
+                expo = jnp.exp(sc - jnp.max(sc, axis=-1, keepdims=True))
+                probs = (expo / jnp.sum(expo, axis=-1, keepdims=True)).astype(jnp.bfloat16)
+                mixed = jnp.dot(
+                    probs, val_ref[pl.ds(0, width), :], preferred_element_type=jnp.float32
+                ).astype(jnp.bfloat16)
+                atb[pl.ds(r * (TILE // block), TILE // block), :, pl.ds(head * HD, HD)] = (
+                    mixed.reshape(TILE // block, block, HD)
+                )
+
+    def d_copy(q, b):
+        return pltpu.make_async_remote_copy(
+            src_ref=sendbuf.at[q, b],
+            dst_ref=got_ref.at[q, i],
+            send_sem=d_send.at[q, b],
+            recv_sem=d_recv.at[q, i],
+            device_id=(g, b, t),
+            device_id_type=MESH,
+        )
+
+    def d_wait(q, b):
+        return pltpu.make_async_remote_copy(
+            src_ref=sendbuf.at[q, b],
+            dst_ref=got_ref.at[q, b],
+            send_sem=d_send.at[q, b],
+            recv_sem=d_recv.at[q, b],
+            device_id=(g, b, t),
+            device_id_type=MESH,
+        )
+
+    def stay(q, b):
+        return pltpu.make_async_copy(sendbuf.at[q, b], got_ref.at[q, b], d_send.at[q, b])
+
+    def l_copy(b):
+        return pltpu.make_async_remote_copy(
+            src_ref=lab_ref.at[b],
+            dst_ref=lab_out.at[i],
+            send_sem=l_send.at[b],
+            recv_sem=l_recv.at[i],
+            device_id=(g, b, t),
+            device_id_type=MESH,
+        )
+
+    def l_wait(b):
+        return pltpu.make_async_remote_copy(
+            src_ref=lab_ref.at[b],
+            dst_ref=lab_out.at[b],
+            send_sem=l_send.at[b],
+            recv_sem=l_recv.at[b],
+            device_id=(g, b, t),
+            device_id_type=MESH,
+        )
+
+    def l_stay(b):
+        return pltpu.make_async_copy(lab_ref.at[b], lab_out.at[b], l_send.at[b])
+
+    def dispatch(q):
+        for b in peers_inst:
+            for k in range(pair):
+                sendbuf[q, b, k] = atb[source_ref[b * pair + k]]
+            start(i != b, functools.partial(d_copy, q, b))
+
+            @pl.when(i == b)
+            def _():
+                stay(q, b).start()
+
+    local[0].wait()
+    start(None, functools.partial(hid_copy, 0, t, t_far))
+    start(None, functools.partial(hid_copy, 1, t, t_core))
+    for copy in local[1:]:
+        copy.wait()
+    send_z(0, 0)
+    send_z(1, 0)
+    for b in peers_inst:
+        start(i != b, functools.partial(l_copy, b))
+
+        @pl.when(i == b)
+        def _():
+            l_stay(b).start()
+
+    send_z(2, 0)
+    comm(0)
+    send_z(3, 0)
+    comm(1)
+    hid_copy(0, t_far, t_far).wait_recv()
+    start(None, functools.partial(hid_copy, 2, t_far, t_core))
+    send_z(4, 0)
+    hid_copy(1, t_core, t_core).wait_recv()
+    hid_copy(2, t_diag, t_core).wait_recv()
+    norm()
+    settle(0)
+    product(0)
+    comm(2)
+    settle(1)
+    product(1)
+    attend()
+    dispatch(0)
+    comm(3)
+    settle(2)
+    product(2)
+    comm(4)
+    attend()
+    dispatch(1)
+    settle(3)
+    product(3)
+    attend()
+    dispatch(2)
+    settle(4)
+    product(4)
+    attend()
+    dispatch(3)
+
+    for b in peers_inst:
+
+        @pl.when(i != b)
+        def _():
+            l_wait(b).wait_recv()
+            for q in range(pieces - 1):
+                d_wait(q, b).wait_recv()
+
+        @pl.when(i == b)
+        def _():
+            l_stay(b).wait()
+            for q in range(pieces - 1):
+                stay(q, b).wait()
+
+    for cond, make in pending:
+        if cond is None:
+            make().wait_send()
+        else:
+
+            @pl.when(cond)
+            def _():
+                make().wait_send()
+
+
+def fused(
+    hidden,
+    norm_gain,
+    w_query,
+    w_key,
+    w_value,
+    bias_query,
+    bias_key,
+    bias_value,
+    prefix_blocks,
+    block_target,
+    cache_slot,
+):
+    owned, block, part = hidden.shape
+    n = lax.axis_size("inst")
+    tp = lax.axis_size("tp")
+    pair = -(-owned // n)
+    tokens = owned * block
+    slots = jnp.arange(owned, dtype=jnp.int32)
+    live = slots < prefix_blocks[0]
+    target = block_target[0]
+    dest = jnp.where(live, target // BAL, -1)
+    place = jnp.where(live, target % BAL, 0)
+    earlier = (dest[:, None] == dest[None, :]) & live[None, :] & (slots[None, :] < slots[:, None])
+    rank = jnp.sum(earlier.astype(jnp.int32), axis=1)
+    item_of_slot = jnp.where(live, dest * pair + rank, -1)
+    items = jnp.arange(n * pair, dtype=jnp.int32)
+    matched = item_of_slot[None, :] == items[:, None]
+    present = jnp.any(matched, axis=1)
+    source = jnp.sum(jnp.where(matched, slots[None, :], 0), axis=1)
+    item_place = jnp.sum(jnp.where(matched, place[None, :], 0), axis=1)
+    label = jnp.where(present, item_place, -1).reshape(n, 1, pair)
+    label = jnp.pad(label, ((0, 0), (0, 7), (0, 128 - pair)), constant_values=-1)
+
+    positions = jnp.arange(tokens, dtype=jnp.int32)
+    freqs = ROPE_BASE ** (-(jnp.arange(HD // 2, dtype=jnp.float32) * 2.0 / HD))
+    angles = positions.astype(jnp.float32)[:, None] * freqs[None, :]
+    cosine, sine = jnp.cos(angles), jnp.sin(angles)
+    cosine = jnp.concatenate([cosine, cosine], axis=1)
+    sine = jnp.concatenate([-sine, sine], axis=1)
+    bias = jnp.concatenate([bias_key, bias_value, bias_query])[None, :]
+
+    rows = w_query.shape[0]
+    heads_cols = w_query.shape[1]
+    pieces = 1 + heads_cols // PIECE
+    any_spec = pl.BlockSpec(memory_space=pl.ANY)
+    vmem = pl.BlockSpec(memory_space=pltpu.VMEM)
+    smem = pl.BlockSpec(memory_space=pltpu.SMEM)
+    dma = pltpu.SemaphoreType.DMA
+    keys, vals, got, got_label = pl.pallas_call(
+        functools.partial(fused_kernel, n, tp, pair),
+        out_shape=[
+            jax.ShapeDtypeStruct((tokens, HD), jnp.bfloat16),
+            jax.ShapeDtypeStruct((tokens, HD), jnp.bfloat16),
+            jax.ShapeDtypeStruct((pieces - 1, n, pair, block, PIECE), jnp.bfloat16),
+            jax.ShapeDtypeStruct((n, 8, 128), jnp.int32),
+        ],
+        in_specs=[smem, any_spec, any_spec, any_spec, any_spec, vmem, vmem, vmem, vmem, any_spec],
+        out_specs=[vmem, vmem, any_spec, any_spec],
+        scratch_shapes=[
+            pltpu.VMEM((tp, tokens, part), jnp.bfloat16),
+            pltpu.VMEM((tokens, tp * part), jnp.bfloat16),
+            pltpu.VMEM((pieces, n * rows, PIECE), jnp.bfloat16),
+            pltpu.VMEM((tokens, PIECE), jnp.bfloat16),
+            pltpu.VMEM((owned, block, PIECE), jnp.bfloat16),
+            pltpu.VMEM((pieces - 1, n, pair, block, PIECE), jnp.bfloat16),
+            dma((pieces + 2,)),
+            dma((3,)),
+            dma((3,)),
+            dma((pieces, 2, n - 1)),
+            dma((pieces, 2, n - 1)),
+            dma((pieces, 2, n - 1)),
+            dma((pieces, 2, n - 1)),
+            dma((pieces - 1, n)),
+            dma((pieces - 1, n)),
+            dma((n,)),
+            dma((n,)),
+        ],
+        compiler_params=pltpu.CompilerParams(
+            collective_id=0, has_side_effects=True, vmem_limit_bytes=56 * 1024 * 1024
+        ),
+    )(
+        source,
+        hidden.reshape(tokens, part),
+        w_query,
+        w_key,
+        w_value,
+        norm_gain[None, :],
+        bias,
+        cosine,
+        sine,
+        label,
+    )
+
+    perm = cache_slot[0]
+    inverse = jnp.sum(jnp.where(perm[None, :] == slots[:, None], slots[None, :], 0), axis=1)
+    zero_half = jnp.zeros((), jnp.bfloat16)
+    live_blocks = (inverse < prefix_blocks[0])[:, None, None]
+    keys = keys.reshape(owned, block, -1)
+    vals = vals.reshape(owned, block, -1)
+    key_cache = jnp.where(live_blocks, jnp.take(keys, inverse, axis=0), zero_half)
+    value_cache = jnp.where(live_blocks, jnp.take(vals, inverse, axis=0), zero_half)
+    labels = got_label[:, 0, :pair].reshape(-1)
+    wanted = labels[None, :] == jnp.arange(BAL, dtype=jnp.int32)[:, None]
+    chosen = jnp.sum(jnp.where(wanted, items[None, :], 0), axis=1)
+    got = got.reshape(pieces - 1, n * pair, block, PIECE)
+    attn_out = jnp.take(got, chosen, axis=1)
+    attn_out = jnp.moveaxis(attn_out, 0, 2).reshape(BAL, block, heads_cols)
+    return (attn_out, key_cache, value_cache)
+
+
 def solution(mesh):
+    small = mesh.shape["inst"] == 4 and mesh.shape["tp"] == 4 and mesh.shape["groups"] == 2
     in_specs = (
         P(("groups", "inst"), None, "tp"),
         P(),
@@ -165,4 +617,5 @@
         P(("groups", "inst"), None, "tp"),
         P(("groups", "inst"), None, "tp"),
     )
-    return jax.shard_map(shards, mesh=mesh, in_specs=in_specs, out_specs=out_specs, check_vma=False)
+    body = fused if small else shards
+    return jax.shard_map(body, mesh=mesh, in_specs=in_specs, out_specs=out_specs, check_vma=False)

time: 405 us -> 172 us (0.42)
  waiting for transfers between devices: 317 us -> 0 us
  Pallas kernels: 0 us -> 156 us
  matrix products: 36.6 us -> 0 us
  between operations: 14.7 us -> 1.43 us
  starting transfers between devices: 10.2 us -> 0 us
  other arithmetic: 14.7 us -> 7.51 us
  local copies, waits for them, and re-layouts: 11.1 us -> 6.85 us
    all_gather x4 -> x0, waiting for transfers between devices: 279 us -> none  [the longest x1 178 us: project(): lax.all_gather(w_query, 'inst', axis=0, tiled=True)]
    pallas_call x0 -> x1, Pallas kernels: none -> 156 us  [fused(): pl.pallas_call(functools.partial(fused_kernel, n, tp, pair), out_shape=[j...]
    dot_general x19 -> x0, matrix products: 36.6 us -> none  [the longest x1 14.6 us: project(): jnp.dot(normed, lax.all_gather(w_query, 'inst', axis=0, tiled=True), pref...]
    all_to_all x2 -> x0, waiting for transfers between devices: 34.9 us -> none  [the longest x1 34.9 us: shards(): lax.all_to_all(send_out, 'inst', split_axis=0, concat_axis=0, tiled=True)]
    all_to_all x2 -> x0, starting transfers between devices: 10 us -> none  [the longest x1 6.32 us: shards(): lax.all_to_all(out_labels, 'inst', split_axis=0, concat_axis=0, tiled=True)]
    reduce_sum x13 -> x4, other arithmetic: 8.31 us -> 1.71 us  [the longest x1 0.77 us: fused(): jnp.sum(jnp.where(perm[None, :] == slots[:, None], slots[None, :], 0), ax...]
  transfers between devices with their start and end apart: 6 -> 0, of which waited for: 5 -> 0; matrix products, arithmetic and copies ran while one was open for 15% -> 0% of each run, Pallas kernels for 0% -> 0%
where the time goes in v1:
time: 172 us
  Pallas kernels  156 us (91%)
  other arithmetic  7.51 us (4%)
  local copies, waits for them, and re-layouts  6.85 us (4%)
    pallas_call x1, Pallas kernels, fused(): pl.pallas_call(functools.partial(fused_kernel, n, tp, pair), out_shape=[j...  156 us

profile of v1, /device:TPU:0, one launch (start us, length us, event | category | flops | bytes accessed | tf_op | source)
XLA Modules:
  0.0 171.9 jit_solution(2719203596293636431)
XLA Ops:
  0.6 0.0 copy-start.1
  0.6 0.0 copy-start.3
  0.7 0.0 copy-start.2
  1.3 0.7 fusion.5
  2.0 0.7 fusion.10
  2.7 0.8 select_reduce_fusion
  3.5 0.2 convert_reduce_fusion
  3.6 0.7 fusion.8
  4.3 0.6 select_reduce_fusion.1
  5.0 0.1 fusion.1
  5.1 0.1 select_n.115
  5.2 0.6 pad.4.lab_ref
  5.8 1.5 fusion
  7.3 1.1 pad_maximum_fusion
  8.4 0.0 copy-done.1
  8.4 0.0 copy-done.3
  8.4 0.0 copy-done.2
  8.4 0.6 broadcast_in_dim.98.bias_ref
  9.0 156.1 %shard_map.130 = (bf16[768,128]{1,0:T(8,128)(2,1)}, bf16[768,128]{1,0:T(8,128)(2,1)}, bf16[4,4,6,32,256]{4,3,2,1,0:T(8,128)(2,1)}, s32[4,8,128]{2,1,0:T(8,128)}) custom-call(s32[24]{0:T(128)} %get-tuple-element.13.source_ref, bf16[768,1280]{1,0:T(8,128)(2,1)} %bitcast.38, bf16[1280,1024]{1,0:T(8,128)(2,1)} %wq_ref.1, bf16[1280,128]{1,0:T(8,128)(2,1)} %wk_ref.1, ...), custom_call_target="tpu_custom_call" | custom-call | tf_op jit(solution)/shard_map/pallas_call | solution.py:538
  165.1 0.0 copy-start
  165.2 1.6 gather_fusion.1
  166.8 1.5 gather_fusion.2
  168.3 0.9 select_select_fusion
  169.2 0.7 slice_reduce_fusion
  169.9 0.1 eq.65
  170.0 0.1 select_reduce_fusion.3
  170.1 0.0 copy-done
  170.1 0.6 gather_fusion
  170.8 0.1 select_bitcast_fusion
  170.9 1.0 copy.20
  (10 shorter events, 0.1 us)
Async XLA Ops:
  0.6 7.8 %copy-start.1 = (f32[1024]{0:T(1024)S(1)}, f32[1024]{0:T(1024)}, u32[]{:S(2)}) copy-start(f32[1024]{0:T(1024)} %param.18) | copy-start | bytes 12292
  0.6 7.8 %copy-start.3 = (f32[128]{0:T(128)S(1)}, f32[128]{0:T(128)}, u32[]{:S(2)}) copy-start(f32[128]{0:T(128)} %param.19) | copy-start | bytes 1540
  0.7 7.8 %copy-start.2 = (f32[128]{0:T(128)S(1)}, f32[128]{0:T(128)}, u32[]{:S(2)}) copy-start(f32[128]{0:T(128)} %param.20) | copy-start | bytes 1540
  165.1 5.0 %copy-start = (bf16[4,4,6,32,256]{4,3,2,1,0:T(8,128)(2,1)S(1)}, bf16[4,4,6,32,256]{4,3,2,1,0:T(8,128)(2,1)}, u32[]{:S(2)}) copy-start(bf16[4,4,6,32,256]{4,3,2,1,0:T(8,128)(2,1)} %get-tuple-element.9) | copy-start | bytes 4718596

commit v2 on v1

--- a/solution.py
+++ b/solution.py
@@ -3,6 +3,7 @@
 
 import jax
 import jax.numpy as jnp
+import numpy as np
 from jax import lax
 from jax.experimental import pallas as pl
 from jax.experimental.pallas import tpu as pltpu
@@ -152,6 +153,11 @@
 TILE = 256
 PIECE = 256
 MESH = pl.DeviceIdType.MESH
+
+
+def cut(slabs):
+    whole = [(k, 0, PIECE) for k in range(slabs - 1)]
+    return whole + [(slabs - 1, 0, HD), (slabs - 1, HD, HD)]
 
 
 def fused_kernel(
@@ -200,7 +206,8 @@
     tokens, part = hid_ref.shape
     rows = wq_ref.shape[0]
     half = rows // 2
-    pieces = wfull.shape[0]
+    parts = cut(wfull.shape[0])
+    pieces = len(parts)
     peers_inst = [b for b in range(n)]
 
     local = [pltpu.make_async_copy(hid_ref, hbuf.at[t], loc_sem.at[0])]
@@ -210,7 +217,9 @@
     for c in range(1, pieces):
         local.append(
             pltpu.make_async_copy(
-                wq_ref.at[:, pl.ds((c - 1) * PIECE, PIECE)], wfull.at[c, own], loc_sem.at[c + 2]
+                wq_ref.at[:, pl.ds((parts[c][0] - 1) * PIECE + parts[c][1], parts[c][2])],
+                wfull.at[parts[c][0], own, pl.ds(parts[c][1], parts[c][2])],
+                loc_sem.at[c + 2],
             )
         )
     for copy in local:
@@ -245,7 +254,9 @@
             make().wait_recv()
 
     def piece(c, j, h):
-        return wfull.at[c, pl.ds(pl.multiple_of(j * rows + h * half, half), half)]
+        slab, off, width = parts[c]
+        here = pl.ds(pl.multiple_of(j * rows + h * half, half), half)
+        return wfull.at[slab, here, pl.ds(off, width)]
 
     def z_copy(c, d, s, j):
         to = i + 1 if d == 0 else i - 1
@@ -282,16 +293,15 @@
         start((i - s >= 0) & (i < n - 1), functools.partial(z_copy, c, 0, s, i - s))
         start((i + s <= n - 1) & (i > 0), functools.partial(z_copy, c, 1, s, i + s))
 
-    def comm(c):
-        for s in range(n - 1):
-            for d in range(2):
-                j = i - 1 - s if d == 0 else i + 1 + s
-                have = j >= 0 if d == 0 else j <= n - 1
-                arrive(have, functools.partial(z_copy, c, d, s, j))
-                if s + 1 < n - 1:
-                    onward = have & ((i < n - 1) if d == 0 else (i > 0))
-                    start(onward, functools.partial(z_copy, c, d, s + 1, j))
-                start(have, functools.partial(y_copy, c, d, s, j, g))
+    def comm(c, s):
+        for d in range(2):
+            j = i - 1 - s if d == 0 else i + 1 + s
+            have = j >= 0 if d == 0 else j <= n - 1
+            arrive(have, functools.partial(z_copy, c, d, s, j))
+            if s + 1 < n - 1:
+                onward = have & ((i < n - 1) if d == 0 else (i > 0))
+                start(onward, functools.partial(z_copy, c, d, s + 1, j))
+            start(have, functools.partial(y_copy, c, d, s, j, g))
 
     def settle(c):
         for s in range(n - 1):
@@ -318,26 +328,33 @@
         return v * cos_ref[here, :] + pltpu.roll(v, HD // 2, 1) * sin_ref[here, :]
 
     def product(c):
+        settle(c)
+        slab, off, width = parts[c]
+
         @pl.loop(0, tokens // TILE)
         def _(r):
             here = pl.ds(pl.multiple_of(r * TILE, TILE), TILE)
-            acc = jnp.dot(normed[here, :], wfull[c], preferred_element_type=jnp.float32)
-            acc = acc + bias_ref[:, pl.ds(c * PIECE, PIECE)]
-            first, second = acc[:, :HD], acc[:, HD:]
+            acc = jnp.dot(
+                normed[here, :],
+                wfull[slab, :, pl.ds(off, width)],
+                preferred_element_type=jnp.float32,
+            )
+            acc = acc + bias_ref[:, pl.ds(slab * PIECE + off, width)]
             if c == 0:
-                key_ref[here, :] = turn(first, here).astype(jnp.bfloat16)
-                val_ref[here, :] = second.astype(jnp.bfloat16)
+                key_ref[here, :] = turn(acc[:, :HD], here).astype(jnp.bfloat16)
+                val_ref[here, :] = acc[:, HD:].astype(jnp.bfloat16)
             else:
-                qbuf[here, pl.ds(0, HD)] = turn(first, here).astype(jnp.bfloat16)
-                qbuf[here, pl.ds(HD, HD)] = turn(second, here).astype(jnp.bfloat16)
-
-    def attend():
+                for head in range(width // HD):
+                    cols = slice(head * HD, (head + 1) * HD)
+                    qbuf[here, cols] = turn(acc[:, cols], here).astype(jnp.bfloat16)
+
+    def attend(c):
         scale = 1.0 / math.sqrt(HD)
         rr = lax.broadcasted_iota(jnp.int32, (TILE, TILE), 0)
         cc = lax.broadcasted_iota(jnp.int32, (TILE, TILE), 1)
         block = atb.shape[1]
         for r in range(tokens // TILE):
-            for head in range(PIECE // HD):
+            for head in range(parts[c][2] // HD):
                 q = qbuf[pl.ds(r * TILE, TILE), pl.ds(head * HD, HD)]
                 width = (r + 1) * TILE
                 sc = (
@@ -360,10 +377,18 @@
                     mixed.reshape(TILE // block, block, HD)
                 )
 
+    def packed(q, b):
+        slab, off, width = parts[q + 1]
+        return sendbuf.at[slab - 1, b, :, :, pl.ds(off, width)]
+
+    def landed(q, b):
+        slab, off, width = parts[q + 1]
+        return got_ref.at[slab - 1, b, :, :, pl.ds(off, width)]
+
     def d_copy(q, b):
         return pltpu.make_async_remote_copy(
-            src_ref=sendbuf.at[q, b],
-            dst_ref=got_ref.at[q, i],
+            src_ref=packed(q, b),
+            dst_ref=landed(q, i),
             send_sem=d_send.at[q, b],
             recv_sem=d_recv.at[q, i],
             device_id=(g, b, t),
@@ -372,8 +397,8 @@
 
     def d_wait(q, b):
         return pltpu.make_async_remote_copy(
-            src_ref=sendbuf.at[q, b],
-            dst_ref=got_ref.at[q, b],
+            src_ref=packed(q, b),
+            dst_ref=landed(q, b),
             send_sem=d_send.at[q, b],
             recv_sem=d_recv.at[q, b],
             device_id=(g, b, t),
@@ -381,7 +406,7 @@
         )
 
     def stay(q, b):
-        return pltpu.make_async_copy(sendbuf.at[q, b], got_ref.at[q, b], d_send.at[q, b])
+        return pltpu.make_async_copy(packed(q, b), landed(q, b), d_send.at[q, b])
 
     def l_copy(b):
         return pltpu.make_async_remote_copy(
@@ -407,9 +432,12 @@
         return pltpu.make_async_copy(lab_ref.at[b], lab_out.at[b], l_send.at[b])
 
     def dispatch(q):
+        slab, off, width = parts[q + 1]
         for b in peers_inst:
             for k in range(pair):
-                sendbuf[q, b, k] = atb[source_ref[b * pair + k]]
+                sendbuf[slab - 1, b, k, :, pl.ds(off, width)] = atb[
+                    source_ref[b * pair + k], :, pl.ds(0, width)
+                ]
             start(i != b, functools.partial(d_copy, q, b))
 
             @pl.when(i == b)
@@ -431,36 +459,36 @@
             l_stay(b).start()
 
     send_z(2, 0)
-    comm(0)
+    last = n - 1
+
+    def comms(c, first=0):
+        for s in range(first, last):
+            comm(c, s)
+
+    comms(0)
     send_z(3, 0)
-    comm(1)
+    comms(1)
     hid_copy(0, t_far, t_far).wait_recv()
     start(None, functools.partial(hid_copy, 2, t_far, t_core))
-    send_z(4, 0)
+    for c in range(4, pieces):
+        send_z(c, 0)
     hid_copy(1, t_core, t_core).wait_recv()
     hid_copy(2, t_diag, t_core).wait_recv()
     norm()
-    settle(0)
+    comm(2, 0)
     product(0)
-    comm(2)
-    settle(1)
-    product(1)
-    attend()
-    dispatch(0)
-    comm(3)
-    settle(2)
-    product(2)
-    comm(4)
-    attend()
-    dispatch(1)
-    settle(3)
-    product(3)
-    attend()
-    dispatch(2)
-    settle(4)
-    product(4)
-    attend()
-    dispatch(3)
+    comms(2, 1)
+    for c in range(1, pieces):
+        ahead = c + 2
+        if ahead < pieces:
+            comm(ahead, 0)
+        product(c)
+        if ahead < pieces:
+            comm(ahead, 1)
+        attend(c)
+        dispatch(c - 1)
+        if ahead < pieces:
+            comms(ahead, 2)
 
     for b in peers_inst:
 
@@ -520,17 +548,18 @@
     label = jnp.where(present, item_place, -1).reshape(n, 1, pair)
     label = jnp.pad(label, ((0, 0), (0, 7), (0, 128 - pair)), constant_values=-1)
 
-    positions = jnp.arange(tokens, dtype=jnp.int32)
-    freqs = ROPE_BASE ** (-(jnp.arange(HD // 2, dtype=jnp.float32) * 2.0 / HD))
-    angles = positions.astype(jnp.float32)[:, None] * freqs[None, :]
-    cosine, sine = jnp.cos(angles), jnp.sin(angles)
-    cosine = jnp.concatenate([cosine, cosine], axis=1)
-    sine = jnp.concatenate([-sine, sine], axis=1)
+    base, power = np.float32(ROPE_BASE), np.arange(HD // 2, dtype=np.float32) * np.float32(2.0 / HD)
+    freqs = np.power(base, -power).astype(np.float32)
+    angles = np.arange(tokens, dtype=np.float32)[:, None] * freqs[None, :]
+    cosine, sine = np.cos(angles), np.sin(angles)
+    cosine = jnp.asarray(np.concatenate([cosine, cosine], axis=1))
+    sine = jnp.asarray(np.concatenate([-sine, sine], axis=1))
     bias = jnp.concatenate([bias_key, bias_value, bias_query])[None, :]
 
     rows = w_query.shape[0]
     heads_cols = w_query.shape[1]
-    pieces = 1 + heads_cols // PIECE
+    slabs = 1 + heads_cols // PIECE
+    pieces = len(cut(slabs))
     any_spec = pl.BlockSpec(memory_space=pl.ANY)
     vmem = pl.BlockSpec(memory_space=pltpu.VMEM)
     smem = pl.BlockSpec(memory_space=pltpu.SMEM)
@@ -540,7 +569,7 @@
         out_shape=[
             jax.ShapeDtypeStruct((tokens, HD), jnp.bfloat16),
             jax.ShapeDtypeStruct((tokens, HD), jnp.bfloat16),
-            jax.ShapeDtypeStruct((pieces - 1, n, pair, block, PIECE), jnp.bfloat16),
+            jax.ShapeDtypeStruct((slabs - 1, n, pair, block, PIECE), jnp.bfloat16),
             jax.ShapeDtypeStruct((n, 8, 128), jnp.int32),
         ],
         in_specs=[smem, any_spec, any_spec, any_spec, any_spec, vmem, vmem, vmem, vmem, any_spec],
@@ -548,10 +577,10 @@
         scratch_shapes=[
             pltpu.VMEM((tp, tokens, part), jnp.bfloat16),
             pltpu.VMEM((tokens, tp * part), jnp.bfloat16),
-            pltpu.VMEM((pieces, n * rows, PIECE), jnp.bfloat16),
+            pltpu.VMEM((slabs, n * rows, PIECE), jnp.bfloat16),
             pltpu.VMEM((tokens, PIECE), jnp.bfloat16),
             pltpu.VMEM((owned, block, PIECE), jnp.bfloat16),
-            pltpu.VMEM((pieces - 1, n, pair, block, PIECE), jnp.bfloat16),
+            pltpu.VMEM((slabs - 1, n, pair, block, PIECE), jnp.bfloat16),
             dma((pieces + 2,)),
             dma((3,)),
             dma((3,)),
@@ -591,7 +620,7 @@
     labels = got_label[:, 0, :pair].reshape(-1)
     wanted = labels[None, :] == jnp.arange(BAL, dtype=jnp.int32)[:, None]
     chosen = jnp.sum(jnp.where(wanted, items[None, :], 0), axis=1)
-    got = got.reshape(pieces - 1, n * pair, block, PIECE)
+    got = got.reshape(slabs - 1, n * pair, block, PIECE)
     attn_out = jnp.take(got, chosen, axis=1)
     attn_out = jnp.moveaxis(attn_out, 0, 2).reshape(BAL, block, heads_cols)
     return (attn_out, key_cache, value_cache)

time: 172 us -> 163 us (0.948)
  Pallas kernels: 156 us -> 149 us
  other arithmetic: 7.51 us -> 5.6 us
    pallas_call x1, Pallas kernels: 156 us -> 149 us  [fused(): pl.pallas_call(functools.partial(fused_kernel, n, tp, pair), out_shape=[j...]
where the time goes in v2:
time: 163 us
  Pallas kernels  149 us (91%)
  local copies, waits for them, and re-layouts  6.84 us (4%)
  other arithmetic  5.6 us (3%)
    pallas_call x1, Pallas kernels, fused(): pl.pallas_call(functools.partial(fused_kernel, n, tp, pair), out_shape=[j...  149 us

profile of v2, /device:TPU:0, one launch (start us, length us, event | category | flops | bytes accessed | tf_op | source)
XLA Modules:
  0.0 162.9 jit_solution(14966545336352039159)
XLA Ops:
  1.3 0.7 fusion.4
  1.9 0.7 fusion.9
  2.6 0.8 select_reduce_fusion
  3.4 0.2 convert_reduce_fusion
  3.6 0.7 fusion.7
  4.3 0.6 select_reduce_fusion.1
  4.9 0.1 fusion
  5.0 0.1 select_n.115
  5.1 0.6 pad.4.lab_ref
  5.7 0.7 pad_maximum_fusion
  6.4 0.6 broadcast_in_dim.96.bias_ref
  7.0 149.1 %shard_map.148 = (bf16[768,128]{1,0:T(8,128)(2,1)}, bf16[768,128]{1,0:T(8,128)(2,1)}, bf16[4,4,6,32,256]{4,3,2,1,0:T(8,128)(2,1)}, s32[4,8,128]{2,1,0:T(8,128)}) custom-call(s32[24]{0:T(128)} %get-tuple-element.13.source_ref, bf16[768,1280]{1,0:T(8,128)(2,1)} %bitcast.38, bf16[1280,1024]{1,0:T(8,128)(2,1)} %wq_ref.1, bf16[1280,128]{1,0:T(8,128)(2,1)} %wk_ref.1, ...), custom_call_target="tpu_custom_call" | custom-call | tf_op jit(solution)/shard_map/pallas_call | solution.py:567
  156.2 0.0 copy-start
  156.2 1.6 gather_fusion.1
  157.8 1.5 gather_fusion.2
  159.4 0.9 select_select_fusion
  160.2 0.7 slice_reduce_fusion
  161.0 0.1 eq.65
  161.0 0.1 select_reduce_fusion.3
  161.2 0.0 copy-done
  161.2 0.6 gather_fusion
  161.8 0.1 select_bitcast_fusion
  162.0 1.0 copy.22
  (7 shorter events, 0.1 us)
Async XLA Ops:
  156.2 5.0 %copy-start = (bf16[4,4,6,32,256]{4,3,2,1,0:T(8,128)(2,1)S(1)}, bf16[4,4,6,32,256]{4,3,2,1,0:T(8,128)(2,1)}, u32[]{:S(2)}) copy-start(bf16[4,4,6,32,256]{4,3,2,1,0:T(8,128)(2,1)} %get-tuple-element.9) | copy-start | bytes 4718596

commit v3 on v2

--- a/solution.py
+++ b/solution.py
@@ -222,7 +222,7 @@
                 loc_sem.at[c + 2],
             )
         )
-    for copy in local:
+    for copy in local[1:3] + local[:1] + local[3:]:
         copy.start()
 
     barrier = pltpu.get_barrier_semaphore()
@@ -444,12 +444,14 @@
             def _():
                 stay(q, b).start()
 
+    local[1].wait()
+    local[2].wait()
+    send_z(0, 0)
     local[0].wait()
     start(None, functools.partial(hid_copy, 0, t, t_far))
     start(None, functools.partial(hid_copy, 1, t, t_core))
-    for copy in local[1:]:
+    for copy in local[3:]:
         copy.wait()
-    send_z(0, 0)
     send_z(1, 0)
     for b in peers_inst:
         start(i != b, functools.partial(l_copy, b))
@@ -483,12 +485,16 @@
         if ahead < pieces:
             comm(ahead, 0)
         product(c)
-        if ahead < pieces:
+        if ahead == pieces:
+            comms(ahead - 1, 2)
+        elif ahead < pieces - 1:
             comm(ahead, 1)
         attend(c)
         dispatch(c - 1)
-        if ahead < pieces:
+        if ahead < pieces - 1:
             comms(ahead, 2)
+        elif ahead == pieces - 1:
+            comm(ahead, 1)
 
     for b in peers_inst:
 

time: 163 us -> 166 us (1.018)
  Pallas kernels: 149 us -> 152 us
    pallas_call x1, Pallas kernels: 149 us -> 152 us  [fused(): pl.pallas_call(functools.partial(fused_kernel, n, tp, pair), out_shape=[j...]
where the time goes in v3:
time: 166 us; the launch traced here: 165 us
  Pallas kernels  152 us (92%)
  local copies, waits for them, and re-layouts  6.84 us (4%)
  other arithmetic  5.6 us (3%)
    pallas_call x1, Pallas kernels, fused(): pl.pallas_call(functools.partial(fused_kernel, n, tp, pair), out_shape=[j...  152 us

profile of v3, /device:TPU:0, one launch (start us, length us, event | category | flops | bytes accessed | tf_op | source)
XLA Modules:
  0.0 165.5 jit_solution(16098018011281730326)
XLA Ops:
  1.3 0.7 fusion.4
  1.9 0.7 fusion.9
  2.6 0.8 select_reduce_fusion
  3.4 0.2 convert_reduce_fusion
  3.6 0.7 fusion.7
  4.3 0.6 select_reduce_fusion.1
  4.9 0.1 fusion
  5.0 0.1 select_n.115
  5.1 0.6 pad.4.lab_ref
  5.7 0.7 pad_maximum_fusion
  6.4 0.6 broadcast_in_dim.96.bias_ref
  7.0 151.7 %shard_map.148 = (bf16[768,128]{1,0:T(8,128)(2,1)}, bf16[768,128]{1,0:T(8,128)(2,1)}, bf16[4,4,6,32,256]{4,3,2,1,0:T(8,128)(2,1)}, s32[4,8,128]{2,1,0:T(8,128)}) custom-call(s32[24]{0:T(128)} %get-tuple-element.13.source_ref, bf16[768,1280]{1,0:T(8,128)(2,1)} %bitcast.38, bf16[1280,1024]{1,0:T(8,128)(2,1)} %wq_ref.1, bf16[1280,128]{1,0:T(8,128)(2,1)} %wk_ref.1, ...), custom_call_target="tpu_custom_call" | custom-call | tf_op jit(solution)/shard_map/pallas_call | solution.py:573
  158.7 0.0 copy-start
  158.8 1.6 gather_fusion.1
  160.4 1.5 gather_fusion.2
  161.9 0.9 select_select_fusion
  162.8 0.7 slice_reduce_fusion
  163.5 0.1 eq.65
  163.6 0.1 select_reduce_fusion.3
  163.7 0.0 copy-done
  163.7 0.6 gather_fusion
  164.4 0.1 select_bitcast_fusion
  164.5 1.0 copy.22
  (7 shorter events, 0.1 us)
Async XLA Ops:
  158.7 5.0 %copy-start = (bf16[4,4,6,32,256]{4,3,2,1,0:T(8,128)(2,1)S(1)}, bf16[4,4,6,32,256]{4,3,2,1,0:T(8,128)(2,1)}, u32[]{:S(2)}) copy-start(bf16[4,4,6,32,256]{4,3,2,1,0:T(8,128)(2,1)} %get-tuple-element.9) | copy-start | bytes 4718596

commit v4 on v2

--- a/solution.py
+++ b/solution.py
@@ -165,6 +165,7 @@
     tp,
     pair,
     source_ref,
+    cache_ref,
     hid_ref,
     wq_ref,
     wk_ref,
@@ -174,10 +175,13 @@
     cos_ref,
     sin_ref,
     lab_ref,
+    key_out,
+    val_out,
+    got_ref,
+    lab_out,
     key_ref,
     val_ref,
-    got_ref,
-    lab_out,
+    kv_blocks,
     hbuf,
     normed,
     wfull,
@@ -341,8 +345,15 @@
             )
             acc = acc + bias_ref[:, pl.ds(slab * PIECE + off, width)]
             if c == 0:
-                key_ref[here, :] = turn(acc[:, :HD], here).astype(jnp.bfloat16)
-                val_ref[here, :] = acc[:, HD:].astype(jnp.bfloat16)
+                k_new = turn(acc[:, :HD], here).astype(jnp.bfloat16)
+                v_new = acc[:, HD:].astype(jnp.bfloat16)
+                key_ref[here, :] = k_new
+                val_ref[here, :] = v_new
+                block = kv_blocks.shape[2]
+                count = TILE // block
+                there = pl.ds(r * count, count)
+                kv_blocks[0, there] = k_new.reshape(count, block, HD)
+                kv_blocks[1, there] = v_new.reshape(count, block, HD)
             else:
                 for head in range(width // HD):
                     cols = slice(head * HD, (head + 1) * HD)
@@ -477,6 +488,11 @@
     norm()
     comm(2, 0)
     product(0)
+    owned = key_out.shape[0]
+    for which, out in enumerate((key_out, val_out)):
+        kv_blocks[which, owned] = jnp.zeros(kv_blocks.shape[2:], jnp.bfloat16)
+        for k in range(owned):
+            out[k] = kv_blocks[which, cache_ref[k]]
     comms(2, 1)
     for c in range(1, pieces):
         ahead = c + 2
@@ -556,6 +572,9 @@
     sine = jnp.asarray(np.concatenate([-sine, sine], axis=1))
     bias = jnp.concatenate([bias_key, bias_value, bias_query])[None, :]
 
+    perm = cache_slot[0]
+    kept = (perm[None, :] == slots[:, None]) & live[None, :]
+    cache_block = owned + jnp.sum(jnp.where(kept, slots[None, :] - owned, 0), axis=1)
     rows = w_query.shape[0]
     heads_cols = w_query.shape[1]
     slabs = 1 + heads_cols // PIECE
@@ -564,17 +583,20 @@
     vmem = pl.BlockSpec(memory_space=pltpu.VMEM)
     smem = pl.BlockSpec(memory_space=pltpu.SMEM)
     dma = pltpu.SemaphoreType.DMA
-    keys, vals, got, got_label = pl.pallas_call(
+    key_cache, value_cache, got, got_label = pl.pallas_call(
         functools.partial(fused_kernel, n, tp, pair),
         out_shape=[
-            jax.ShapeDtypeStruct((tokens, HD), jnp.bfloat16),
-            jax.ShapeDtypeStruct((tokens, HD), jnp.bfloat16),
+            jax.ShapeDtypeStruct((owned, block, HD), jnp.bfloat16),
+            jax.ShapeDtypeStruct((owned, block, HD), jnp.bfloat16),
             jax.ShapeDtypeStruct((slabs - 1, n, pair, block, PIECE), jnp.bfloat16),
             jax.ShapeDtypeStruct((n, 8, 128), jnp.int32),
         ],
-        in_specs=[smem, any_spec, any_spec, any_spec, any_spec, vmem, vmem, vmem, vmem, any_spec],
+        in_specs=[smem, smem, any_spec, any_spec, any_spec, any_spec, vmem, vmem, vmem, vmem, any_spec],
         out_specs=[vmem, vmem, any_spec, any_spec],
         scratch_shapes=[
+            pltpu.VMEM((tokens, HD), jnp.bfloat16),
+            pltpu.VMEM((tokens, HD), jnp.bfloat16),
+            pltpu.VMEM((2, owned + 1, block, HD), jnp.bfloat16),
             pltpu.VMEM((tp, tokens, part), jnp.bfloat16),
             pltpu.VMEM((tokens, tp * part), jnp.bfloat16),
             pltpu.VMEM((slabs, n * rows, PIECE), jnp.bfloat16),
@@ -598,6 +620,7 @@
         ),
     )(
         source,
+        cache_block,
         hidden.reshape(tokens, part),
         w_query,
         w_key,
@@ -609,14 +632,6 @@
         label,
     )
 
-    perm = cache_slot[0]
-    inverse = jnp.sum(jnp.where(perm[None, :] == slots[:, None], slots[None, :], 0), axis=1)
-    zero_half = jnp.zeros((), jnp.bfloat16)
-    live_blocks = (inverse < prefix_blocks[0])[:, None, None]
-    keys = keys.reshape(owned, block, -1)
-    vals = vals.reshape(owned, block, -1)
-    key_cache = jnp.where(live_blocks, jnp.take(keys, inverse, axis=0), zero_half)
-    value_cache = jnp.where(live_blocks, jnp.take(vals, inverse, axis=0), zero_half)
     labels = got_label[:, 0, :pair].reshape(-1)
     wanted = labels[None, :] == jnp.arange(BAL, dtype=jnp.int32)[:, None]
     chosen = jnp.sum(jnp.where(wanted, items[None, :], 0), axis=1)

time: 163 us -> 162 us (level)
    gather x2 -> x0, local copies, waits for them, and re-layouts: 3.13 us -> none  [the longest x1 1.62 us: fused(): jnp.take(keys, inverse, axis=0)]
where the time goes in v4:
time: 162 us
  Pallas kernels  149 us (92%)
  local copies, waits for them, and re-layouts  6.46 us (4%)
  other arithmetic  5.18 us (3%)
    pallas_call x1, Pallas kernels, fused(): pl.pallas_call(functools.partial(fused_kernel, n, tp, pair), out_shape=[j...  149 us

profile of v4, /device:TPU:0, one launch (start us, length us, event | category | flops | bytes accessed | tf_op | source)
XLA Modules:
  0.0 162.1 jit_solution(11055139128069292255)
XLA Ops:
  1.3 0.7 fusion.5
  2.0 0.7 fusion.10
  2.6 0.8 select_reduce_fusion.1
  3.5 0.6 broadcast_add_fusion.cache_ref
  4.1 0.7 fusion.8
  4.7 0.1 fusion
  4.8 0.6 select_reduce_fusion
  5.5 0.1 select_n.103
  5.6 0.7 pad_maximum_fusion
  6.3 0.6 broadcast_in_dim.74.bias_ref
  6.9 0.6 pad.4.lab_ref
  7.5 149.1 %shard_map.148 = (bf16[24,32,128]{2,1,0:T(8,128)(2,1)}, bf16[24,32,128]{2,1,0:T(8,128)(2,1)}, bf16[4,4,6,32,256]{4,3,2,1,0:T(8,128)(2,1)}, s32[4,8,128]{2,1,0:T(8,128)}) custom-call(s32[24]{0:T(128)} %get-tuple-element.12.source_ref, s32[24]{0:T(128)} %broadcast_add_fusion.cache_ref, bf16[768,1280]{1,0:T(8,128)(2,1)} %bitcast.36, bf16[1280,1024]{1,0:T(8,128)(2,1)} %wq_ref.1, ...), custom_call_target="tpu_custom_call" | custom-call | tf_op jit(solution)/shard_map/pallas_call | solution.py:586
  156.6 0.7 slice_reduce_fusion
  157.4 0.1 eq.68
  157.4 0.1 select_reduce_fusion.3
  157.6 2.0 %gather_fusion = bf16[12,4,32,256]{3,2,1,0:T(8,128)(2,1)S(1)} fusion(bf16[4,24,32,256]{3,2,1,0:T(8,128)(2,1)} %bitcast.38, s32[1024]{0:T(1024)S(1)} %pad_clamp_fusion), kind=kCustom, calls=%fused_computation | custom fusion | bytes 1572912 | tf_op jit(solution)/shard_map/jit(_take)/gather | solution.py:639
  159.6 0.0 copy-start.1
  159.6 0.0 copy-start
  159.6 0.1 select_bitcast_fusion
  159.8 1.0 copy.20
  160.7 0.0 copy-done.1
  160.8 0.7 copy.24
  161.4 0.0 copy-done
  161.4 0.7 copy.25
  (5 shorter events, 0.0 us)
Async XLA Ops:
  159.6 1.1 copy-start.1
  159.6 1.8 %copy-start = (bf16[24,32,128]{2,1,0:T(8,128)(2,1)S(1)}, bf16[24,32,128]{2,1,0:T(8,128)(2,1)}, u32[]{:S(2)}) copy-start(bf16[24,32,128]{2,1,0:T(8,128)(2,1)} %get-tuple-element.25) | copy-start | bytes 589828
